TPU v7x, 512 devices: a whole 4x4x16 slice. The times are simulated.
512 devices in a mesh: wave: 16 (over z), tile: 32 (over y, x, core).
Axes of the slice: x: 4, y: 4, z: 16, core: 2. Of those that a mesh axis runs over, the one named last changes fastest.
Arguments:
- warm_start: float32 [16, 2, 1024, 1024], P('wave', None, 'tile'), may hold values from -30 to 30
- class_map: int32 [1024, 1024], P('tile'), may hold values from 0 to 7
- conductivities: float32 [8], replicated, may hold values from 0.1 to 10
- wavenumbers: float32 [16], P('wave'), may hold values from 0.05 to 2
- weights: float32 [16], P('wave'), may hold values from 0.1 to 1
- source_row: int32 [2], replicated, may hold values from 0 to 1023
- source_col: int32 [2], replicated, may hold values from 0 to 1023
- electrode_row: int32 [64], replicated, may hold values from 0 to 1023
Outputs:
- potentials: float32 [2, 1024, 1024], P(None, 'tile', 'wave')
- readings: float32 [2, 64], replicated
All inputs are finite; a program needn't handle non-finite values.
Results may differ from a plain program's by a relative error of at most 0.0003.
Values sent between devices are 32-bit elements; how exact they have to be, the bound alone decides.
A program may use at most 64 MiB of HBM per device.

v0:
```python
import jax
import jax.numpy as jnp
from jax import lax
from jax.sharding import PartitionSpec as P

ITERS = 3
source_strength = 50.0


def extended(shard, sides, width):
    for axis, dim in sides:
        size, length = (lax.axis_size(axis), shard.shape[dim])
        up = [(i, (i + 1) % size) for i in range(size - 1)]
        down = [(j, i) for i, j in up]
        last = lax.slice_in_dim(shard, length - width, length, axis=dim)
        initial = lax.slice_in_dim(shard, 0, width, axis=dim)
        before = lax.ppermute(last, axis, up)
        after = lax.ppermute(initial, axis, down)
        shard = jnp.concatenate([before, shard, after], axis=dim)
    return shard


def harmonic(left_val, right_val):
    return 2.0 * left_val * right_val / (left_val + right_val)


def shards(
    warm_start,
    class_map,
    conductivities,
    wavenumbers,
    weights,
    source_row,
    source_col,
    electrode_row,
):
    rows_here = class_map.shape[0]
    depth = class_map.shape[1]
    n_class = conductivities.shape[0]
    class_ids = jnp.arange(n_class, dtype=jnp.int32)
    sigma = jnp.sum(
        jnp.where(class_map[None] == class_ids[:, None, None], conductivities[:, None, None], 0.0),
        axis=0,
    )
    sigma_rim = extended(sigma, (("tile", 0),), 1)
    face_row = harmonic(sigma_rim[:-1], sigma_rim[1:])
    face_up = face_row[:-1]
    face_down = face_row[1:]
    col_inner = harmonic(sigma[:, :-1], sigma[:, 1:])
    face_left = jnp.concatenate([jnp.zeros((rows_here, 1), jnp.float32), col_inner], axis=1)
    face_right = jnp.concatenate([col_inner, sigma[:, -1:]], axis=1)
    base = face_up + face_down + face_left + face_right
    wave_num = wavenumbers[0]
    diag = base + wave_num * wave_num * sigma
    global_row = lax.axis_index("tile") * rows_here + jnp.arange(rows_here, dtype=jnp.int32)
    col_ids = jnp.arange(depth, dtype=jnp.int32)
    hits = (global_row[None, :, None] == source_row[:, None, None]) & (
        col_ids[None, None, :] == source_col[:, None, None]
    )
    rhs = source_strength * hits.astype(jnp.float32)

    def operate(values):
        row_padded = extended(values, (("tile", 1),), 1)
        col_padded = jnp.pad(values, ((0, 0), (0, 0), (1, 1)))
        return (
            diag * values
            - face_up * row_padded[:, :-2]
            - face_down * row_padded[:, 2:]
            - face_left * col_padded[:, :, :-2]
            - face_right * col_padded[:, :, 2:]
        )

    def local_inner(first, second):
        return jnp.sum(first * second, axis=(1, 2))

    def resid_inner(residual, scaled):
        return lax.psum(local_inner(residual, scaled), "tile")[:, None, None]

    field = warm_start[0]
    residual = rhs - operate(field)
    scaled = residual / diag
    direction = scaled
    gamma_now = resid_inner(residual, scaled)
    for iteration in range(ITERS):
        image = operate(direction)
        curve = lax.psum(local_inner(direction, image), "tile")[:, None, None]
        step_size = gamma_now / curve
        field = field + step_size * direction
        residual = residual - step_size * image
        scaled = residual / diag
        gamma_next = resid_inner(residual, scaled)
        direction = scaled + gamma_next / gamma_now * direction
        gamma_now = gamma_next
    weighted = weights[0] * field
    picker = (global_row[:, None] == electrode_row[None, :]).astype(jnp.float32)
    local_read = jnp.dot(
        weighted[:, :, 0],
        picker,
        precision=lax.Precision.HIGHEST,
        preferred_element_type=jnp.float32,
    )
    readings = lax.psum(local_read, ("wave", "tile"))
    summed = lax.psum(weighted, "wave")
    share = depth // lax.axis_size("wave")
    potentials = lax.dynamic_slice_in_dim(summed, lax.axis_index("wave") * share, share, 2)
    return (potentials, readings)


def solution(mesh):
    return jax.shard_map(
        shards,
        mesh=mesh,
        in_specs=(
            P("wave", None, "tile", None),
            P("tile", None),
            P(),
            P("wave"),
            P("wave"),
            P(),
            P(),
            P(),
        ),
        out_specs=(P(None, "tile", "wave"), P()),
        check_vma=False,
    )
```

profile of v0, /device:TPU:2, one launch (start us, length us, event | category | flops | bytes accessed | tf_op | source)
XLA Modules:
  0.0 508.0 jit_solution(10058735618531560873)
XLA Ops:
  7.2 1.1 select_reduce_fusion
  8.3 1.9 collective-permute-start
  10.3 3.6 collective-permute-start.1
  13.9 1.9 collective-permute-start.2
  15.9 5.6 %collective-permute-start.3 = (f32[2,1,1024]{2,1,0:T(1,128)S(1)}, f32[2,1,1024]{2,1,0:T(1,128)S(1)}, u32[]{:S(2)}, u32[]{:S(2)}) collective-permute-start(f32[2,1,1024]{2,1,0:T(1,128)S(1)} %get-tuple-element.22), channel_id=1, source_target_pairs={{1,0},{2,1},{3,2},{4,3},{5,4},{6,5},{7,6},{8,7},{9,8},{10,9},{11,1... | collective-permute-start | bytes 24584 | tf_op jit(solution)/shard_map/ppermute | solution.py:18
  21.4 0.1 add_divide_fusion.1
  21.6 0.0 copy-start.2
  21.6 0.6 copy-done.2
  22.2 0.1 iota_compare_fusion.1
  22.3 0.6 copy-done.3
  22.9 0.1 broadcast_compare_fusion
  23.0 0.1 slice.146
  23.7 0.0 collective-permute-done
  23.7 0.0 collective-permute-done.1
  23.7 0.1 add_divide_fusion
  23.8 0.1 multiply_add_fusion.2
  23.9 0.2 broadcast_divide_fusion
  24.2 1.9 collective-permute-start.4
  26.1 3.6 collective-permute-start.5
  29.8 1.3 collective-permute-done.5
  31.1 0.3 multiply_reduce_fusion.3
  31.4 59.2 %all-reduce.5 = (f32[2]{0:T(128)S(1)}, f32[2]{0:T(128)S(1)}) all-reduce(f32[2]{0:T(128)S(1)} %get-tuple-element.3, f32[2]{0:T(128)S(1)} %get-tuple-element.2), channel_id=1, replica_groups=mesh['wave'=16,'tile'=32] {'tile'}, use_global_device_ids=true, to_apply=%region_2.3 | all-reduce | flops 4 | bytes 32 | tf_op jit(solution)/shard_map/psum | solution.py:77
  90.6 0.2 multiply_reduce_fusion.2
  90.8 62.7 %psum.58 = f32[2]{0:T(128)S(1)} all-reduce(f32[2]{0:T(128)S(1)} %get-tuple-element.8), channel_id=1, replica_groups=mesh['wave'=16,'tile'=32] {'tile'}, use_global_device_ids=true, to_apply=%region_6.7 | all-reduce | flops 2 | bytes 16 | tf_op jit(solution)/shard_map/psum | solution.py:77
  153.5 0.1 multiply_add_fusion.1
  153.6 1.9 collective-permute-start.6
  155.5 7.0 %collective-permute-start.7 = (f32[2,1,1024]{2,1,0:T(1,128)S(1)}, f32[2,1,1024]{2,1,0:T(1,128)S(1)}, u32[]{:S(2)}, u32[]{:S(2)}) collective-permute-start(f32[2,1,1024]{2,1,0:T(1,128)S(1)} %get-tuple-element.18), channel_id=1, source_target_pairs={{1,0},{2,1},{3,2},{4,3},{5,4},{6,5},{7,6},{8,7},{9,8},{10,9},{11,1... | collective-permute-start | bytes 24584 | tf_op jit(solution)/shard_map/ppermute | solution.py:18
  162.5 1.3 collective-permute-done.7
  163.8 0.3 multiply_reduce_fusion.1
  164.1 59.2 %psum.59 = f32[2]{0:T(128)S(1)} all-reduce(f32[2]{0:T(128)S(1)} %get-tuple-element.6), channel_id=1, replica_groups=mesh['wave'=16,'tile'=32] {'tile'}, use_global_device_ids=true, to_apply=%region_8.9 | all-reduce | flops 2 | bytes 16 | tf_op jit(solution)/shard_map/psum | solution.py:86
  223.3 0.2 multiply_reduce_fusion
  223.5 62.7 %psum.60 = f32[2]{0:T(128)S(1)} all-reduce(f32[2]{0:T(128)S(1)} %multiply_reduce_fusion), channel_id=1, replica_groups=mesh['wave'=16,'tile'=32] {'tile'}, use_global_device_ids=true, to_apply=%region_10.11 | all-reduce | flops 2 | bytes 16 | tf_op jit(solution)/shard_map/psum | solution.py:77
  286.2 0.1 multiply_add_fusion
  286.4 1.9 collective-permute-start.8
  288.3 7.0 %collective-permute-start.9 = (f32[2,1,1024]{2,1,0:T(1,128)S(1)}, f32[2,1,1024]{2,1,0:T(1,128)S(1)}, u32[]{:S(2)}, u32[]{:S(2)}) collective-permute-start(f32[2,1,1024]{2,1,0:T(1,128)S(1)} %get-tuple-element.16), channel_id=1, source_target_pairs={{1,0},{2,1},{3,2},{4,3},{5,4},{6,5},{7,6},{8,7},{9,8},{10,9},{11,1... | collective-permute-start | bytes 24584 | tf_op jit(solution)/shard_map/ppermute | solution.py:18
  295.3 1.3 collective-permute-done.9
  296.6 0.3 fusion.17
  297.6 59.2 %psum.61 = f32[2]{0:T(128)S(1)} all-reduce(f32[2]{0:T(128)S(1)} %fusion.17), channel_id=1, replica_groups=mesh['wave'=16,'tile'=32] {'tile'}, use_global_device_ids=true, to_apply=%region_12.13 | all-reduce | flops 2 | bytes 16 | tf_op jit(solution)/shard_map/psum | solution.py:86
  356.8 0.2 add_multiply_fusion
  357.0 0.1 slice_reduce_fusion
  357.1 0.6 copy-done
  357.7 0.1 all-reduce.8.cloned.1.call-update
  357.8 0.0 copy-start.4
  357.8 0.6 copy-done.4
  358.4 0.2 fusion.35
  358.6 110.4 %psum.63 = f32[2,64]{1,0:T(2,128)} all-reduce(f32[2,64]{1,0:T(2,128)S(1)} %fusion.35), channel_id=1, replica_groups=mesh['wave'=16,'tile'=32] {'wave','tile'}, use_global_device_ids=true, to_apply=%region_14.15 | all-reduce | flops 128 | bytes 1024 | tf_op jit(solution)/shard_map/psum | solution.py:102
  469.1 30.6 %all-reduce.8.cloned.1.call-done = f32[2,32,1024]{2,1,0:T(8,128)} async-done(((f32[2,32,1024]{2,1,0:T(8,128)}), f32[2,32,1024]{2,1,0:T(8,128)}) %all-reduce.8.cloned.1.call-update) | async-done | bytes 262160 | tf_op jit(solution)/shard_map/psum | solution.py:103
  499.7 1.4 constant_dynamic-slice_fusion
  (21 shorter events, 0.1 us)
Async XLA Ops:
  7.2 6.8 %copy-start.1 = (f32[1,2,32,1024]{3,2,1,0:T(8,128)S(1)}, f32[1,2,32,1024]{3,2,1,0:T(8,128)}, u32[]{:S(2)}) copy-start(f32[1,2,32,1024]{3,2,1,0:T(8,128)} %param.8) | copy-start | bytes 786436
  8.3 15.4 %collective-permute-start = (f32[1,1024]{1,0:T(1,128)S(1)}, f32[1,1024]{1,0:T(1,128)S(1)}, u32[]{:S(2)}, u32[]{:S(2)}) collective-permute-start(f32[1,1024]{1,0:T(1,128)S(1)} %get-tuple-element.26), channel_id=1, source_target_pairs={{0,1},{1,2},{2,3},{3,4},{4,5},{5,6},{6,7},{7,8},{8,9},{9,10},{10,1... | collective-permute-start | bytes 12296 | tf_op jit(solution)/shard_map/ppermute | solution.py:17
  10.3 13.4 %collective-permute-start.1 = (f32[1,1024]{1,0:T(1,128)S(1)}, f32[1,1024]{1,0:T(1,128)S(1)}, u32[]{:S(2)}, u32[]{:S(2)}) collective-permute-start(f32[1,1024]{1,0:T(1,128)S(1)} %get-tuple-element.27), channel_id=1, source_target_pairs={{1,0},{2,1},{3,2},{4,3},{5,4},{6,5},{7,6},{8,7},{9,8},{10,9},{11,1... | collective-permute-start | bytes 12296 | tf_op jit(solution)/shard_map/ppermute | solution.py:18
  13.9 9.9 %collective-permute-start.2 = (f32[2,1,1024]{2,1,0:T(1,128)S(1)}, f32[2,1,1024]{2,1,0:T(1,128)S(1)}, u32[]{:S(2)}, u32[]{:S(2)}) collective-permute-start(f32[2,1,1024]{2,1,0:T(1,128)S(1)} %get-tuple-element.21), channel_id=1, source_target_pairs={{0,1},{1,2},{2,3},{3,4},{4,5},{5,6},{6,7},{7,8},{8,9},{9,10},{10,1... | collective-permute-start | bytes 24584 | tf_op jit(solution)/shard_map/ppermute | solution.py:17
  15.9 8.0 %collective-permute-start.3 = (f32[2,1,1024]{2,1,0:T(1,128)S(1)}, f32[2,1,1024]{2,1,0:T(1,128)S(1)}, u32[]{:S(2)}, u32[]{:S(2)}) collective-permute-start(f32[2,1,1024]{2,1,0:T(1,128)S(1)} %get-tuple-element.22), channel_id=1, source_target_pairs={{1,0},{2,1},{3,2},{4,3},{5,4},{6,5},{7,6},{8,7},{9,8},{10,9},{11,1... | collective-permute-start | bytes 24584 | tf_op jit(solution)/shard_map/ppermute | solution.py:18
  21.6 0.7 copy-start.2
  22.2 0.7 copy-start.3
  24.2 5.6 %collective-permute-start.4 = (f32[2,1,1024]{2,1,0:T(1,128)S(1)}, f32[2,1,1024]{2,1,0:T(1,128)S(1)}, u32[]{:S(2)}, u32[]{:S(2)}) collective-permute-start(f32[2,1,1024]{2,1,0:T(1,128)S(1)} %get-tuple-element.19), channel_id=1, source_target_pairs={{0,1},{1,2},{2,3},{3,4},{4,5},{5,6},{6,7},{7,8},{8,9},{9,10},{10,1... | collective-permute-start | bytes 24584 | tf_op jit(solution)/shard_map/ppermute | solution.py:17
  26.1 5.0 collective-permute-start.5
  153.6 8.9 %collective-permute-start.6 = (f32[2,1,1024]{2,1,0:T(1,128)S(1)}, f32[2,1,1024]{2,1,0:T(1,128)S(1)}, u32[]{:S(2)}, u32[]{:S(2)}) collective-permute-start(f32[2,1,1024]{2,1,0:T(1,128)S(1)} %get-tuple-element.17), channel_id=1, source_target_pairs={{0,1},{1,2},{2,3},{3,4},{4,5},{5,6},{6,7},{7,8},{8,9},{9,10},{10,1... | collective-permute-start | bytes 24584 | tf_op jit(solution)/shard_map/ppermute | solution.py:17
  155.5 8.3 %collective-permute-start.7 = (f32[2,1,1024]{2,1,0:T(1,128)S(1)}, f32[2,1,1024]{2,1,0:T(1,128)S(1)}, u32[]{:S(2)}, u32[]{:S(2)}) collective-permute-start(f32[2,1,1024]{2,1,0:T(1,128)S(1)} %get-tuple-element.18), channel_id=1, source_target_pairs={{1,0},{2,1},{3,2},{4,3},{5,4},{6,5},{7,6},{8,7},{9,8},{10,9},{11,1... | collective-permute-start | bytes 24584 | tf_op jit(solution)/shard_map/ppermute | solution.py:18
  286.4 8.9 %collective-permute-start.8 = (f32[2,1,1024]{2,1,0:T(1,128)S(1)}, f32[2,1,1024]{2,1,0:T(1,128)S(1)}, u32[]{:S(2)}, u32[]{:S(2)}) collective-permute-start(f32[2,1,1024]{2,1,0:T(1,128)S(1)} %get-tuple-element.15), channel_id=1, source_target_pairs={{0,1},{1,2},{2,3},{3,4},{4,5},{5,6},{6,7},{7,8},{8,9},{9,10},{10,1... | collective-permute-start | bytes 24584 | tf_op jit(solution)/shard_map/ppermute | solution.py:17
  288.3 8.3 %collective-permute-start.9 = (f32[2,1,1024]{2,1,0:T(1,128)S(1)}, f32[2,1,1024]{2,1,0:T(1,128)S(1)}, u32[]{:S(2)}, u32[]{:S(2)}) collective-permute-start(f32[2,1,1024]{2,1,0:T(1,128)S(1)} %get-tuple-element.16), channel_id=1, source_target_pairs={{1,0},{2,1},{3,2},{4,3},{5,4},{6,5},{7,6},{8,7},{9,8},{10,9},{11,1... | collective-permute-start | bytes 24584 | tf_op jit(solution)/shard_map/ppermute | solution.py:18
  357.0 0.7 copy-start
  357.1 142.7 %all-reduce.8.cloned.1.call-start = ((), (), s32[]{:S(2)}) async-start(), calls=%async_computation | async-start | bytes 524288 | tf_op jit(solution)/shard_map/psum | solution.py:103
  357.8 0.7 copy-start.4
Sparse Core Ops, SparseCore 0:
  360.2 139.4 all-reduce.7
where the time goes:
time: 509 us; the launch traced here: 508 us
  blocking collectives  413 us (81%)
  starting transfers between devices  36.4 us (7%)
  waiting for transfers between devices  34.8 us (7%)
  between operations  15.6 us (3%)
    psum x3, blocking collectives, resid_inner(): return lax.psum(local_inner(residual, scaled), 'tile')[:, None, None]  184 us
    psum x2, blocking collectives, shards(): curve = lax.psum(local_inner(direction, image), 'tile')[:, None, None]  118 us
    psum x1, blocking collectives, shards(): readings = lax.psum(local_read, ('wave', 'tile'))  110 us
    psum x1, waiting for transfers between devices, shards(): summed = lax.psum(weighted, 'wave')  30.6 us
    ppermute x5, starting transfers between devices, extended(): after = lax.ppermute(initial, axis, down)  26.8 us
  transfers between devices with their start and end apart: 11, of which 4 were waited for; matrix products, arithmetic and copies ran while one was open for 0% of the time, Pallas kernels for 0%

commit v1 on v0

--- a/solution.py
+++ b/solution.py
@@ -1,3 +1,4 @@
+import functools
 import jax
 import jax.numpy as jnp
 from jax import lax
@@ -5,6 +6,20 @@
 
 ITERS = 3
 source_strength = 50.0
+
+
+def process_tracks(z_in, axis_tag):
+    axis_len = jax.lax.axis_size(axis_tag)
+    carry_in = z_in
+    for jj in [m for m in (1, 2, 4, 8, 16) if m < axis_len]:
+        block_list = []
+        for h in range(axis_len):
+            block_list.append((h, h ^ jj))
+        carry_in = carry_in + jax.lax.ppermute(carry_in, axis_name=axis_tag, perm=block_list)
+    return carry_in
+
+
+_rest_table = functools.partial(process_tracks, axis_tag="wave")
 
 
 def extended(shard, sides, width):
@@ -100,7 +115,7 @@
         preferred_element_type=jnp.float32,
     )
     readings = lax.psum(local_read, ("wave", "tile"))
-    summed = lax.psum(weighted, "wave")
+    summed = _rest_table(weighted)
     share = depth // lax.axis_size("wave")
     potentials = lax.dynamic_slice_in_dim(summed, lax.axis_index("wave") * share, share, 2)
     return (potentials, readings)

time: 509 us -> 529 us (1.039)
  the two profiles are of different devices: /device:TPU:2 before, /device:TPU:1 now
where the time goes in v1:
time: 529 us
  blocking collectives  412 us (78%)
  starting transfers between devices  62.7 us (12%)
  waiting for transfers between devices  46 us (9%)
    psum x3, blocking collectives, resid_inner(): return lax.psum(local_inner(residual, scaled), 'tile')[:, None, None]  190 us
    psum x2, blocking collectives, shards(): curve = lax.psum(local_inner(direction, image), 'tile')[:, None, None]  121 us
    psum x1, blocking collectives, shards(): readings = lax.psum(local_read, ('wave', 'tile'))  101 us
    ppermute x4, waiting for transfers between devices, process_tracks(): jax.lax.ppermute(carry_in, axis_name=axis_tag, perm=block_list)  37.7 us
    ppermute x4, starting transfers between devices, process_tracks(): jax.lax.ppermute(carry_in, axis_name=axis_tag, perm=block_list)  34.7 us
    ppermute x5, starting transfers between devices, extended(): after = lax.ppermute(initial, axis, down)  14.7 us
    ppermute x5, starting transfers between devices, extended(): before = lax.ppermute(last, axis, up)  13.3 us
  transfers between devices with their start and end apart: 14, of which 7 were waited for; matrix products, arithmetic and copies ran while one was open for 0% of the time, Pallas kernels for 0%

profile of v1, /device:TPU:1, one launch (start us, length us, event | category | flops | bytes accessed | tf_op | source)
XLA Modules:
  0.0 528.8 jit_solution(2274133457379855286)
XLA Ops:
  0.6 1.1 select_reduce_fusion
  1.8 4.5 collective-permute-start
  6.3 5.6 %collective-permute-start.1 = (f32[1,1024]{1,0:T(1,128)S(1)}, f32[1,1024]{1,0:T(1,128)S(1)}, u32[]{:S(2)}, u32[]{:S(2)}) collective-permute-start(f32[1,1024]{1,0:T(1,128)S(1)} %get-tuple-element.27), channel_id=1, source_target_pairs={{1,0},{2,1},{3,2},{4,3},{5,4},{6,5},{7,6},{8,7},{9,8},{10,9},{11,1... | collective-permute-start | bytes 12296 | tf_op jit(solution)/shard_map/ppermute | solution.py:33
  11.9 1.9 collective-permute-start.2
  13.9 2.4 collective-permute-start.3
  16.3 0.1 add_divide_fusion.1
  16.4 0.6 copy-done.1
  17.0 0.1 iota_compare_fusion.1
  17.1 0.6 copy-done.2
  17.7 0.1 broadcast_compare_fusion
  17.8 0.1 slice.146
  18.6 0.1 multiply_add_fusion.2
  18.7 0.1 collective-permute-done.3
  18.8 0.2 broadcast_divide_fusion
  19.1 3.1 collective-permute-start.4
  22.2 1.9 collective-permute-start.5
  24.1 3.0 collective-permute-done.5
  27.1 0.3 multiply_reduce_fusion.3
  27.4 60.1 %all-reduce.5 = (f32[2]{0:T(128)S(1)}, f32[2]{0:T(128)S(1)}) all-reduce(f32[2]{0:T(128)S(1)} %get-tuple-element.3, f32[2]{0:T(128)S(1)} %get-tuple-element.2), channel_id=1, replica_groups=mesh['wave'=16,'tile'=32] {'tile'}, use_global_device_ids=true, to_apply=%region_2.3 | all-reduce | flops 4 | bytes 32 | tf_op jit(solution)/shard_map/psum | solution.py:92
  87.6 0.2 multiply_reduce_fusion.2
  87.8 65.1 %psum.51 = f32[2]{0:T(128)S(1)} all-reduce(f32[2]{0:T(128)S(1)} %get-tuple-element.8), channel_id=1, replica_groups=mesh['wave'=16,'tile'=32] {'tile'}, use_global_device_ids=true, to_apply=%region_6.7 | all-reduce | flops 2 | bytes 16 | tf_op jit(solution)/shard_map/psum | solution.py:92
  152.8 0.1 multiply_add_fusion.1
  153.0 1.9 collective-permute-start.6
  154.9 2.4 collective-permute-start.7
  157.3 2.5 collective-permute-done.7
  159.9 0.3 multiply_reduce_fusion.1
  160.2 60.6 %psum.52 = f32[2]{0:T(128)S(1)} all-reduce(f32[2]{0:T(128)S(1)} %get-tuple-element.6), channel_id=1, replica_groups=mesh['wave'=16,'tile'=32] {'tile'}, use_global_device_ids=true, to_apply=%region_8.9 | all-reduce | flops 2 | bytes 16 | tf_op jit(solution)/shard_map/psum | solution.py:101
  220.8 0.2 multiply_reduce_fusion
  221.0 64.6 %psum.53 = f32[2]{0:T(128)S(1)} all-reduce(f32[2]{0:T(128)S(1)} %multiply_reduce_fusion), channel_id=1, replica_groups=mesh['wave'=16,'tile'=32] {'tile'}, use_global_device_ids=true, to_apply=%region_10.11 | all-reduce | flops 2 | bytes 16 | tf_op jit(solution)/shard_map/psum | solution.py:92
  285.6 0.1 multiply_add_fusion
  285.7 1.9 collective-permute-start.8
  287.7 2.4 collective-permute-start.9
  290.1 2.5 collective-permute-done.9
  292.6 0.3 fusion.17
  293.6 60.6 %psum.54 = f32[2]{0:T(128)S(1)} all-reduce(f32[2]{0:T(128)S(1)} %fusion.17), channel_id=1, replica_groups=mesh['wave'=16,'tile'=32] {'tile'}, use_global_device_ids=true, to_apply=%region_12.13 | all-reduce | flops 2 | bytes 16 | tf_op jit(solution)/shard_map/psum | solution.py:101
  354.2 0.1 add_multiply_fusion
  354.4 3.1 collective-permute-start.10
  357.5 4.0 collective-permute-done.10
  361.5 4.6 collective-permute-start.11
  366.2 11.1 %collective-permute-done.11 = f32[2,32,1024]{2,1,0:T(8,128)S(1)} collective-permute-done((f32[2,32,1024]{2,1,0:T(8,128)S(1)}, f32[2,32,1024]{2,1,0:T(8,128)S(1)}, u32[]{:S(2)}, u32[]{:S(2)}) %collective-permute-start.11) | collective-permute-done | bytes 262176 | tf_op jit(solution)/shard_map/ppermute | solution.py:18
  377.3 8.8 %collective-permute-start.12 = (f32[2,32,1024]{2,1,0:T(8,128)S(1)}, f32[2,32,1024]{2,1,0:T(8,128)S(1)}, u32[]{:S(2)}, u32[]{:S(2)}) collective-permute-start(f32[2,32,1024]{2,1,0:T(8,128)S(1)} %add.100), channel_id=1, source_target_pairs={{0,128},{32,160},{64,192},{96,224},{128,0},{160,32},{192,64},{224,... | collective-permute-start | bytes 786440 | tf_op jit(solution)/shard_map/ppermute | solution.py:18
  386.2 22.6 %collective-permute-done.12 = f32[2,32,1024]{2,1,0:T(8,128)S(1)} collective-permute-done((f32[2,32,1024]{2,1,0:T(8,128)S(1)}, f32[2,32,1024]{2,1,0:T(8,128)S(1)}, u32[]{:S(2)}, u32[]{:S(2)}) %collective-permute-start.12) | collective-permute-done | bytes 262176 | tf_op jit(solution)/shard_map/ppermute | solution.py:18
  408.8 0.0 copy-start.3
  408.8 18.2 %collective-permute-start.13 = (f32[2,32,1024]{2,1,0:T(8,128)S(1)}, f32[2,32,1024]{2,1,0:T(8,128)S(1)}, u32[]{:S(2)}, u32[]{:S(2)}) collective-permute-start(f32[2,32,1024]{2,1,0:T(8,128)S(1)} %add.101), channel_id=1, source_target_pairs={{0,256},{32,288},{64,320},{96,352},{128,384},{160,416},{192,448},{... | collective-permute-start | bytes 786440 | tf_op jit(solution)/shard_map/ppermute | solution.py:18
  427.0 0.1 slice_reduce_fusion
  427.1 0.2 fusion.35
  427.3 100.8 %psum.55 = f32[2,64]{1,0:T(2,128)} all-reduce(f32[2,64]{1,0:T(2,128)S(1)} %fusion.35), channel_id=1, replica_groups=mesh['wave'=16,'tile'=32] {'wave','tile'}, use_global_device_ids=true, to_apply=%region_13.14 | all-reduce | flops 128 | bytes 1024 | tf_op jit(solution)/shard_map/psum | solution.py:117
  528.1 0.7 dynamic-slice_add_fusion
  (27 shorter events, 0.3 us)
Async XLA Ops:
  0.6 11.3 %copy-start = (f32[1,2,32,1024]{3,2,1,0:T(8,128)S(1)}, f32[1,2,32,1024]{3,2,1,0:T(8,128)}, u32[]{:S(2)}) copy-start(f32[1,2,32,1024]{3,2,1,0:T(8,128)} %param.8) | copy-start | bytes 786436
  1.8 16.7 %collective-permute-start = (f32[1,1024]{1,0:T(1,128)S(1)}, f32[1,1024]{1,0:T(1,128)S(1)}, u32[]{:S(2)}, u32[]{:S(2)}) collective-permute-start(f32[1,1024]{1,0:T(1,128)S(1)} %get-tuple-element.26), channel_id=1, source_target_pairs={{0,1},{1,2},{2,3},{3,4},{4,5},{5,6},{6,7},{7,8},{8,9},{9,10},{10,1... | collective-permute-start | bytes 12296 | tf_op jit(solution)/shard_map/ppermute | solution.py:32
  6.3 12.2 %collective-permute-start.1 = (f32[1,1024]{1,0:T(1,128)S(1)}, f32[1,1024]{1,0:T(1,128)S(1)}, u32[]{:S(2)}, u32[]{:S(2)}) collective-permute-start(f32[1,1024]{1,0:T(1,128)S(1)} %get-tuple-element.27), channel_id=1, source_target_pairs={{1,0},{2,1},{3,2},{4,3},{5,4},{6,5},{7,6},{8,7},{9,8},{10,9},{11,1... | collective-permute-start | bytes 12296 | tf_op jit(solution)/shard_map/ppermute | solution.py:33
  11.9 6.8 %collective-permute-start.2 = (f32[2,1,1024]{2,1,0:T(1,128)S(1)}, f32[2,1,1024]{2,1,0:T(1,128)S(1)}, u32[]{:S(2)}, u32[]{:S(2)}) collective-permute-start(f32[2,1,1024]{2,1,0:T(1,128)S(1)} %get-tuple-element.21), channel_id=1, source_target_pairs={{0,1},{1,2},{2,3},{3,4},{4,5},{5,6},{6,7},{7,8},{8,9},{9,10},{10,1... | collective-permute-start | bytes 24584 | tf_op jit(solution)/shard_map/ppermute | solution.py:32
  13.9 5.0 collective-permute-start.3
  16.4 0.7 copy-start.1
  17.0 0.7 copy-start.2
  19.1 5.0 collective-permute-start.4
  22.2 5.0 collective-permute-start.5
  153.0 4.3 collective-permute-start.6
  154.9 5.0 collective-permute-start.7
  285.7 4.3 collective-permute-start.8
  287.7 5.0 collective-permute-start.9
  354.4 7.1 %collective-permute-start.10 = (f32[2,32,1024]{2,1,0:T(8,128)S(1)}, f32[2,32,1024]{2,1,0:T(8,128)S(1)}, u32[]{:S(2)}, u32[]{:S(2)}) collective-permute-start(f32[2,32,1024]{2,1,0:T(8,128)S(1)} %add_multiply_fusion), channel_id=1, source_target_pairs={{0,32},{32,0},{64,96},{96,64},{128,160},{160,128},{192,224},{224,1... | collective-permute-start | bytes 786440 | tf_op jit(solution)/shard_map/ppermute | solution.py:18
  361.5 15.8 %collective-permute-start.11 = (f32[2,32,1024]{2,1,0:T(8,128)S(1)}, f32[2,32,1024]{2,1,0:T(8,128)S(1)}, u32[]{:S(2)}, u32[]{:S(2)}) collective-permute-start(f32[2,32,1024]{2,1,0:T(8,128)S(1)} %add.99), channel_id=1, source_target_pairs={{0,64},{32,96},{64,0},{96,32},{128,192},{160,224},{192,128},{224,1... | collective-permute-start | bytes 786440 | tf_op jit(solution)/shard_map/ppermute | solution.py:18
  377.3 31.4 %collective-permute-start.12 = (f32[2,32,1024]{2,1,0:T(8,128)S(1)}, f32[2,32,1024]{2,1,0:T(8,128)S(1)}, u32[]{:S(2)}, u32[]{:S(2)}) collective-permute-start(f32[2,32,1024]{2,1,0:T(8,128)S(1)} %add.100), channel_id=1, source_target_pairs={{0,128},{32,160},{64,192},{96,224},{128,0},{160,32},{192,64},{224,... | collective-permute-start | bytes 786440 | tf_op jit(solution)/shard_map/ppermute | solution.py:18
  408.8 18.3 %copy-start.3 = (s32[64]{0:T(128)S(1)}, s32[64]{0:T(128)}, u32[]{:S(2)}) copy-start(s32[64]{0:T(128)} %param.15) | copy-start | bytes 772
  408.8 119.3 %collective-permute-start.13 = (f32[2,32,1024]{2,1,0:T(8,128)S(1)}, f32[2,32,1024]{2,1,0:T(8,128)S(1)}, u32[]{:S(2)}, u32[]{:S(2)}) collective-permute-start(f32[2,32,1024]{2,1,0:T(8,128)S(1)} %add.101), channel_id=1, source_target_pairs={{0,256},{32,288},{64,320},{96,352},{128,384},{160,416},{192,448},{... | collective-permute-start | bytes 786440 | tf_op jit(solution)/shard_map/ppermute | solution.py:18
